TPU v7x, 32 devices: a whole 2x2x4 slice. The times are simulated.
32 devices in a mesh: tm: 4 (over y, core), dp: 8 (over z, x).
Axes of the slice: x: 2, y: 2, z: 4, core: 2. Of those that a mesh axis runs over, the one named last changes fastest.
Arguments:
- tokens: bfloat16 [8, 8, 64, 1152], P('dp', 'tm'), may hold values from -6 to 6
- clip_frames: int32 [8, 4], P('dp'), may hold values from 1 to 4, 8 in all within a row
- teacher_scores: float32 [8, 4, 8], P('dp'), may hold values from -4 to 4
- ln_gain: float32 [1152], replicated, may hold values from 0.25 to 1.75
- w_qkv: bfloat16 [1152, 3456], replicated, may hold values from -1 to 1
- w_out: bfloat16 [1152, 1152], replicated, may hold values from -0.1875 to 0.1875
- out_gain: float32 [1152], replicated, may hold values from 0.25 to 1.75
- reward_head: float32 [1152, 8], replicated, may hold values from -1.8856181 to 1.8856181
Outputs:
- scores: float32 [8, 4, 8], P('dp')
- grad_qkv: float32 [1152, 3456], P('dp')
- grad_out: float32 [1152, 1152], P('dp')
Inputs may be any that keep to these rules, and one draw needn't show every extreme that they name: `clip_frames`: each row lists the lengths of 4 clips laid end to end over its 8 frames; the longest clip of every row has exactly 4 frames.
All inputs are finite; a program needn't handle non-finite values.
Results may differ from a plain program's by a relative error of at most 0.033.
Values may be sent and summed in bfloat16 or wider, within the bound.
A program may use at most 128 MiB of HBM per device.

v0:
```python
import math

import jax
import jax.numpy as jnp
from jax import lax
from jax.experimental import pallas as pl
from jax.experimental.pallas import tpu as pltpu
from jax.sharding import PartitionSpec as P

HEADS = 16
HEAD_DIM = 72
WINDOW = 8
LANES = 128


norm_eps = 1e-06
highest = lax.Precision.HIGHEST
score_scale = 1.0 / math.sqrt(HEAD_DIM)


def swapped(block, axis, bit):
    route = [(i, i ^ (1 << bit)) for i in range(lax.axis_size(axis))]
    return lax.ppermute(block, axis, route)


def layer_norm(values, gain_vector):
    centre = values - jnp.mean(values, axis=-1, keepdims=True)
    inv_std = lax.rsqrt(jnp.mean(centre * centre, axis=-1, keepdims=True) + norm_eps)
    normal_form = centre * inv_std
    return (normal_form * gain_vector, normal_form, inv_std)


def dot_nt(left, right):
    return lax.dot_general(
        left, right, (((1,), (1,)), ((), ())), preferred_element_type=jnp.float32
    )


def dot_tn(left, right):
    return lax.dot_general(
        left, right, (((0,), (0,)), ((), ())), preferred_element_type=jnp.float32
    )


def head_lanes(head):
    first, last = head * HEAD_DIM, (head + 1) * HEAD_DIM
    start = first // LANES * LANES
    stop = -(-last // LANES) * LANES
    lane = lax.broadcasted_iota(jnp.int32, (1, stop - start), 1) + start
    return start, stop, (lane >= first) & (lane < last)


def forward_kernel(projected_ref, allowed_ref, attended_ref, weights_ref, total):
    width = attended_ref.shape[1]
    total[...] = jnp.zeros_like(total)
    allowed = allowed_ref[...] > 0
    for head in range(HEADS):
        start, stop, own = head_lanes(head)
        query = projected_ref[:, start:stop]
        key = projected_ref[:, width + start : width + stop]
        value = projected_ref[:, 2 * width + start : 2 * width + stop]
        query = jnp.where(own, query, jnp.zeros_like(query))
        logits = jnp.where(allowed, dot_nt(query, key) * score_scale, -1e30)
        terms = jnp.exp(logits - jnp.max(logits, axis=1, keepdims=True))
        weights = terms / jnp.sum(terms, axis=1, keepdims=True)
        weights_ref[head] = weights
        mixed = jnp.dot(weights.astype(jnp.bfloat16), value, preferred_element_type=jnp.float32)
        total[:, start:stop] += jnp.where(own, mixed, 0.0)
    attended_ref[...] = total[...].astype(jnp.bfloat16)


def backward_kernel(projected_ref, weights_ref, grad_ref, out_ref, total):
    width = grad_ref.shape[1]
    total[...] = jnp.zeros_like(total)
    for head in range(HEADS):
        start, stop, own = head_lanes(head)
        query = projected_ref[:, start:stop]
        key = projected_ref[:, width + start : width + stop]
        value = projected_ref[:, 2 * width + start : 2 * width + stop]
        grad = grad_ref[:, start:stop]
        grad = jnp.where(own, grad, jnp.zeros_like(grad))
        weights = weights_ref[head]
        weight_grad = dot_nt(grad, value)
        mean_grad = jnp.sum(weights * weight_grad, axis=1, keepdims=True)
        logit_grad = (weights * (weight_grad - mean_grad)).astype(jnp.bfloat16)
        query_grad = jnp.dot(logit_grad, key, preferred_element_type=jnp.float32)
        key_grad = dot_tn(logit_grad, query)
        value_grad = dot_tn(weights.astype(jnp.bfloat16), grad)
        total[:, start:stop] += jnp.where(own, query_grad * score_scale, 0.0)
        total[:, width + start : width + stop] += jnp.where(own, key_grad * score_scale, 0.0)
        total[:, 2 * width + start : 2 * width + stop] += value_grad
    out_ref[...] = total[...].astype(jnp.bfloat16)


def attend(projected, allowed):
    count, width = projected.shape[0], projected.shape[1] // 3
    return pl.pallas_call(
        forward_kernel,
        out_shape=(
            jax.ShapeDtypeStruct((count, width), jnp.bfloat16),
            jax.ShapeDtypeStruct((HEADS, count, count), jnp.float32),
        ),
        in_specs=[pl.BlockSpec(memory_space=pltpu.VMEM)] * 2,
        out_specs=[pl.BlockSpec(memory_space=pltpu.VMEM)] * 2,
        scratch_shapes=[pltpu.VMEM((count, width), jnp.float32)],
        compiler_params=pltpu.CompilerParams(vmem_limit_bytes=24 * 1024 * 1024),
    )(projected, allowed)


def attend_grad(projected, weights, attended_grad):
    return pl.pallas_call(
        backward_kernel,
        out_shape=jax.ShapeDtypeStruct(projected.shape, jnp.bfloat16),
        in_specs=[pl.BlockSpec(memory_space=pltpu.VMEM)] * 3,
        out_specs=pl.BlockSpec(memory_space=pltpu.VMEM),
        scratch_shapes=[pltpu.VMEM(projected.shape, jnp.float32)],
        compiler_params=pltpu.CompilerParams(vmem_limit_bytes=24 * 1024 * 1024),
    )(projected, weights, attended_grad)


def summed_blocks(normed, attended, grads):
    n_tm, n_dp = lax.axis_size("tm"), lax.axis_size("dp")
    me_tm, me_dp = lax.axis_index("tm"), lax.axis_index("dp")
    count, width = normed.shape
    rows = width // n_dp
    columns = grads.shape[1] // n_tm
    first_out = n_tm * 3 // 4
    order = me_dp ^ jnp.arange(n_dp, dtype=jnp.int32)

    def relative_rows(values):
        blocks = jnp.take(values.T.reshape(n_dp, rows, count), order, axis=0)
        return blocks.reshape(width, count)

    left_qkv, left_out = relative_rows(normed), relative_rows(attended)
    pieces = 3
    piece = columns // pieces
    bits_tm, bits_dp = n_tm.bit_length() - 1, n_dp.bit_length() - 1
    lead = [("tm", 1), ("dp", 0), ("dp", 1)]
    rest = [("dp", b) for b in range(2, bits_dp)] + [("tm", b) for b in range(2, bits_tm)]
    steps = [[("tm", 0)] + lead[i:] + lead[:i] + rest for i in range(pieces)]

    def product(part, number):
        block = me_tm ^ number
        left = jnp.where(block < first_out, left_qkv, left_out)
        right = lax.dynamic_slice(grads, (0, block * columns + part * piece), (count, piece))
        full = jnp.dot(left, right, preferred_element_type=jnp.float32)
        return full.astype(jnp.bfloat16).reshape(n_dp, rows, piece)

    held = [{} for _ in range(pieces)]
    numbers = [list(range(n_tm)) for _ in range(pieces)]
    for part in range(pieces):
        for number in sorted(range(n_tm), key=lambda r: (1 - (r & 1), r)):
            held[part][number] = product(part, number)
    for at in range(len(steps[0])):
        for part in range(pieces):
            axis, bit = steps[part][at]
            blocks = held[part]
            if axis == "tm":
                going = [r for r in blocks if (r >> bit) & 1]
                for r in going:
                    other = swapped(blocks.pop(r), "tm", bit)
                    kept = r ^ (1 << bit)
                    total = blocks[kept].astype(jnp.float32) + other.astype(jnp.float32)
                    blocks[kept] = total.astype(jnp.bfloat16)
            else:
                for r in blocks:
                    done = sum(1 for a, b in steps[part][:at] if a == "dp" and b < bit)
                    size = 1 << (bit - done)
                    rank = blocks[r].shape[0] // (2 * size)
                    pair = blocks[r].reshape(rank, 2, size, rows, piece)
                    kept = pair[:, 0].reshape(rank * size, rows, piece)
                    going = pair[:, 1].reshape(rank * size, rows, piece)
                    other = swapped(going, "dp", bit)
                    total = kept.astype(jnp.float32) + other.astype(jnp.float32)
                    blocks[r] = total.astype(jnp.bfloat16)
    mine = jnp.concatenate([held[part][0][0] for part in range(pieces)], axis=1)
    gathered = mine[None]
    for bit in reversed(range(bits_tm)):
        gathered = jnp.concatenate([gathered, swapped(gathered, "tm", bit)], axis=0)
    place = []
    for number in range(n_tm):
        place.append(sum(((number >> b) & 1) << (bits_tm - 1 - b) for b in range(bits_tm)))
    place = jnp.array(place, dtype=jnp.int32)
    whole = []
    for block in range(n_tm):
        whole.append(lax.dynamic_index_in_dim(gathered, place[me_tm ^ block], 0, keepdims=False))
    qkv = jnp.concatenate(whole[:first_out], axis=1).astype(jnp.float32)
    out = jnp.concatenate(whole[first_out:], axis=1).astype(jnp.float32)
    return qkv, out


def on_device(tokens, clip_frames, teacher_scores, ln_gain, w_qkv, w_out, out_gain, reward_head):
    width = tokens.shape[3]
    n_tm = lax.axis_size("tm")
    row_count = lax.axis_size("dp")
    positions = tokens.shape[2]
    inputs = lax.all_to_all(tokens[0], "tm", split_axis=1, concat_axis=0, tiled=True)
    frames, own_positions = inputs.shape[0], inputs.shape[1]
    count = frames * own_positions
    inputs = inputs.reshape(count, width).astype(jnp.float32)
    lengths = clip_frames[0]
    index = jnp.arange(count, dtype=jnp.int32)
    frame, position = index // own_positions, index % own_positions
    clip = jnp.sum((jnp.cumsum(lengths)[None, :] <= frame[:, None]).astype(jnp.int32), axis=1)
    lag = frame[None, :] - frame[:, None]
    behind = WINDOW // 2
    allowed = (
        (position[None, :] == position[:, None])
        & (clip[None, :] == clip[:, None])
        & (lag >= -behind)
        & (lag < WINDOW - behind)
    )
    normed_full, _, _ = layer_norm(inputs, ln_gain)
    normed = normed_full.astype(jnp.bfloat16)
    projected = jnp.dot(normed, w_qkv, preferred_element_type=jnp.float32).astype(jnp.bfloat16)
    attended, weights = attend(projected, allowed.astype(jnp.float32))
    mixed = inputs + jnp.dot(attended, w_out, preferred_element_type=jnp.float32)
    final_norm, centred, inv_std = layer_norm(mixed, out_gain)
    per_token = jnp.dot(final_norm, reward_head, precision=highest)
    onehot = (clip[:, None] == jnp.arange(lengths.shape[0], dtype=jnp.int32)[None, :]).astype(
        jnp.float32
    )
    clip_totals = jnp.dot(onehot.T, per_token, precision=highest)
    for bit in range(n_tm.bit_length() - 1):
        clip_totals = clip_totals + swapped(clip_totals, "tm", bit)
    counts = lengths.astype(jnp.float32) * positions
    scores = clip_totals / counts[:, None]
    residue = (scores - teacher_scores[0]) / row_count
    clip_grad = jnp.dot(residue, reward_head.T, precision=highest) * out_gain
    scaled = jnp.dot(onehot, clip_grad, precision=highest)
    mixed_grad = (
        scaled
        - jnp.mean(scaled, axis=-1, keepdims=True)
        - centred * jnp.mean(scaled * centred, axis=-1, keepdims=True)
    ) * inv_std
    mixed_grad = mixed_grad.astype(jnp.bfloat16)
    attended_grad = dot_nt(mixed_grad, w_out).astype(jnp.bfloat16)
    projected_grad = attend_grad(projected, weights, attended_grad)
    grads = jnp.concatenate([projected_grad, mixed_grad], axis=1)
    qkv_total, out_total = summed_blocks(normed, attended, grads)
    return (scores[None], qkv_total, out_total)


def solution(mesh):
    return jax.shard_map(
        on_device,
        mesh=mesh,
        in_specs=(
            P("dp", "tm", None, None),
            P("dp", None),
            P("dp", None, None),
            P(),
            P(),
            P(),
            P(),
            P(),
        ),
        out_specs=(P("dp", None, None), P("dp", None), P("dp", None)),
        check_vma=False,
    )
```

profile of v0, /device:TPU:1, one launch (start us, length us, event | category | flops | bytes accessed | tf_op | source)
XLA Modules:
  0.0 152.8 jit_solution(11321369938926837561)
XLA Ops:
  0.6 2.1 %copy.104 = bf16[1,2,64,1152]{3,1,2,0:T(2,128)(2,1)} copy(bf16[1,2,64,1152]{3,2,1,0:T(8,128)(2,1)} %param.11) | data formatting | bytes 589824 | tf_op args[0]
  2.8 4.4 %all-to-all-start = ((bf16[2,64,1152]{2,0,1:T(2,128)(2,1)}), bf16[2,64,1152]{2,0,1:T(2,128)(2,1)S(1)}, u32[]{:S(2)}, u32[]{:S(2)}) async-start(bf16[2,64,1152]{2,0,1:T(2,128)(2,1)} %bitcast.228), calls=%async_computation | async-start | bytes 589824 | tf_op jit(solution)/shard_map/all_to_all | solution.py:197
  7.2 0.6 compare_and_fusion
  7.8 0.8 reduce-window.8
  8.7 0.7 fusion.61.allowed_ref
  9.5 1.2 multiply_bitcast_fusion
  10.6 1.9 %all-to-all-done = bf16[2,64,1152]{2,0,1:T(2,128)(2,1)S(1)} async-done(((bf16[2,64,1152]{2,0,1:T(2,128)(2,1)}), bf16[2,64,1152]{2,0,1:T(2,128)(2,1)S(1)}, u32[]{:S(2)}, u32[]{:S(2)}) %all-to-all-start) | async-done | bytes 294944 | tf_op jit(solution)/shard_map/all_to_all | solution.py:197
  13.1 0.6 div.49
  13.9 0.7 copy-done.7
  14.6 0.8 fusion.13
  15.4 4.7 %convolution_convert_fusion.projected_ref = bf16[128,3456]{1,0:T(8,128)(2,1)S(1)} fusion(bf16[128,1152]{1,0:T(8,128)(2,1)S(1)} %fusion.13, bf16[1152,3456]{1,0:T(8,128)(2,1)} %param.15), kind=kOutput, calls=%fused_computation.2 | convolution fusion | flops 1019658240 | bytes 9142272 | tf_op jit(solution)/shard_map/dot_general | solution.py:215
  20.2 3.4 %shard_map.112 = (bf16[128,1152]{1,0:T(8,128)(2,1)S(1)}, f32[16,128,128]{2,1,0:T(8,128)S(1)}) custom-call(bf16[128,3456]{1,0:T(8,128)(2,1)S(1)} %convolution_convert_fusion.projected_ref, f32[128,128]{1,0:T(8,128)S(1)} %copy-done.4), custom_call_target="tpu_custom_call" | custom-call | tf_op jit(solution)/shard_map/pallas_call | solution.py:97
  23.6 0.7 fusion.100
  24.9 0.6 copy-done.5
  25.5 0.7 fusion.16
  26.2 0.9 fusion.64
  27.0 1.0 collective-permute-start
  28.0 1.8 %copy.70 = bf16[1152,128]{1,0:T(8,128)(2,1)} copy(bf16[1152,128]{0,1:T(8,128)(2,1)} %bitcast.243) | data formatting | bytes 589824 | tf_op jit(solution)/shard_map/transpose | solution.py:131
  29.9 1.8 %copy.71 = bf16[1152,128]{1,0:T(8,128)(2,1)} copy(bf16[1152,128]{0,1:T(8,128)(2,1)} %bitcast.229) | data formatting | bytes 589824 | tf_op jit(solution)/shard_map/transpose | solution.py:131
  31.7 2.2 %gather_fusion = bf16[8,144,128]{2,1,0:T(8,128)(2,1)} fusion(bf16[8,144,128]{2,1,0:T(8,128)(2,1)} %bitcast.268, s32[1024]{0:T(1024)S(1)} %pad_clamp_fusion), kind=kCustom, calls=%fused_computation.clone | custom fusion | bytes 589856 | tf_op jit(solution)/shard_map/jit(_take)/gather | solution.py:131
  34.0 2.3 %gather_fusion.1 = bf16[8,144,128]{2,1,0:T(8,128)(2,1)} fusion(bf16[8,144,128]{2,1,0:T(8,128)(2,1)} %bitcast.267, s32[1024]{0:T(1024)S(1)} %pad_clamp_fusion), kind=kCustom, calls=%fused_computation.1.clone | custom fusion | bytes 589856 | tf_op jit(solution)/shard_map/jit(_take)/gather | solution.py:131
  36.3 0.8 add.220
  37.1 1.2 broadcast_select_fusion.4
  38.3 1.1 collective-permute-done.1
  39.4 0.7 add_divide_fusion
  40.1 0.9 convolution_multiply_fusion
  41.0 1.3 fusion.96
  42.6 0.9 convolution_convert_fusion.13.grad_ref
  43.8 5.1 %shard_map.113 = bf16[128,3456]{1,0:T(8,128)(2,1)S(1)} custom-call(bf16[128,3456]{1,0:T(8,128)(2,1)S(1)} %convolution_convert_fusion.projected_ref, f32[16,128,128]{2,1,0:T(8,128)S(1)} %copy-done.3, bf16[128,1152]{1,0:T(8,128)(2,1)S(1)} %convolution_convert_fusion.13.grad_ref), custom_call_target="tpu_custom_call" | custom-call | tf_op jit(solution)/shard_map/pallas_call | solution.py:111
  49.3 1.2 collective-permute-start.18
  51.4 0.4 convolution_convert_fusion.6
  52.3 0.6 collective-permute-start.11
  53.2 0.6 convolution_convert_fusion.8
  53.8 0.4 convolution_convert_fusion.7
  54.7 0.6 collective-permute-start.3
  55.6 0.4 convolution_convert_fusion.11
  56.1 0.4 convolution_convert_fusion.12
  56.9 2.0 %collective-permute-start.19 = (bf16[4,144,384]{2,1,0:T(8,128)(2,1)S(1)}, bf16[4,144,384]{2,1,0:T(8,128)(2,1)S(1)}, u32[]{:S(2)}, u32[]{:S(2)}) collective-permute-start(bf16[4,144,384]{2,1,0:T(8,128)(2,1)S(1)} %bitcast.276), channel_id=1, source_target_pairs={{0,2},{1,3},{2,0},{3,1},{4,6},{5,7},{6,4},{7,5},{8,10},{9,11},{10,... | collective-permute-start | bytes 1327112 | tf_op jit(solution)/shard_map/ppermute | solution.py:23
  59.7 1.4 collective-permute-start.12
  61.8 7.2 %collective-permute-done.19 = bf16[4,144,384]{2,1,0:T(8,128)(2,1)S(1)} collective-permute-done((bf16[4,144,384]{2,1,0:T(8,128)(2,1)S(1)}, bf16[4,144,384]{2,1,0:T(8,128)(2,1)S(1)}, u32[]{:S(2)}, u32[]{:S(2)}) %collective-permute-start.19) | collective-permute-done | bytes 442400 | tf_op jit(solution)/shard_map/ppermute | solution.py:23
  69.3 1.4 collective-permute-done.12
  70.9 9.3 %collective-permute-done.9 = bf16[4,144,384]{2,1,0:T(8,128)(2,1)S(1)} collective-permute-done((bf16[4,144,384]{2,1,0:T(8,128)(2,1)S(1)}, bf16[4,144,384]{2,1,0:T(8,128)(2,1)S(1)}, u32[]{:S(2)}, u32[]{:S(2)}) %collective-permute-start.9) | collective-permute-done | bytes 442400 | tf_op jit(solution)/shard_map/ppermute | solution.py:23
  80.2 1.1 collective-permute-start.13
  81.4 4.0 %collective-permute-done.13 = bf16[2,144,384]{2,1,0:T(8,128)(2,1)S(1)} collective-permute-done((bf16[2,144,384]{2,1,0:T(8,128)(2,1)S(1)}, bf16[2,144,384]{2,1,0:T(8,128)(2,1)S(1)}, u32[]{:S(2)}, u32[]{:S(2)}) %collective-permute-start.13) | collective-permute-done | bytes 221216 | tf_op jit(solution)/shard_map/ppermute | solution.py:23
  85.4 0.9 collective-permute-start.10
  86.6 11.4 %collective-permute-done.20 = bf16[4,144,384]{2,1,0:T(8,128)(2,1)S(1)} collective-permute-done((bf16[4,144,384]{2,1,0:T(8,128)(2,1)S(1)}, bf16[4,144,384]{2,1,0:T(8,128)(2,1)S(1)}, u32[]{:S(2)}, u32[]{:S(2)}) %collective-permute-start.20) | collective-permute-done | bytes 442400 | tf_op jit(solution)/shard_map/ppermute | solution.py:23
  98.3 0.5 collective-permute-start.21
  98.8 4.0 %collective-permute-done.14 = bf16[2,144,384]{2,1,0:T(8,128)(2,1)S(1)} collective-permute-done((bf16[2,144,384]{2,1,0:T(8,128)(2,1)S(1)}, bf16[2,144,384]{2,1,0:T(8,128)(2,1)S(1)}, u32[]{:S(2)}, u32[]{:S(2)}) %collective-permute-start.14) | collective-permute-done | bytes 221216 | tf_op jit(solution)/shard_map/ppermute | solution.py:23
  102.9 1.6 %collective-permute-start.15 = (bf16[1,144,384]{2,1,0:T(8,128)(2,1)S(1)}, bf16[1,144,384]{2,1,0:T(8,128)(2,1)S(1)}, u32[]{:S(2)}, u32[]{:S(2)}) collective-permute-start(bf16[1,144,384]{2,1,0:T(8,128)(2,1)S(1)} %slice_bitcast_fusion.16), channel_id=1, source_target_pairs={{0,4},{1,5},{2,6},{3,7},{4,0},{5,1},{6,2},{7,3},{8,12},{9,13},{10,... | collective-permute-start | bytes 331784 | tf_op jit(solution)/shard_map/ppermute | solution.py:23
  104.9 1.3 collective-permute-start.5
  106.1 2.5 %collective-permute-done.15 = bf16[1,144,384]{2,1,0:T(8,128)(2,1)S(1)} collective-permute-done((bf16[1,144,384]{2,1,0:T(8,128)(2,1)S(1)}, bf16[1,144,384]{2,1,0:T(8,128)(2,1)S(1)}, u32[]{:S(2)}, u32[]{:S(2)}) %collective-permute-start.15) | collective-permute-done | bytes 110624 | tf_op jit(solution)/shard_map/ppermute | solution.py:23
  108.7 6.3 %collective-permute-done.5 = bf16[4,144,384]{2,1,0:T(8,128)(2,1)S(1)} collective-permute-done((bf16[4,144,384]{2,1,0:T(8,128)(2,1)S(1)}, bf16[4,144,384]{2,1,0:T(8,128)(2,1)S(1)}, u32[]{:S(2)}, u32[]{:S(2)}) %collective-permute-start.5) | collective-permute-done | bytes 442400 | tf_op jit(solution)/shard_map/ppermute | solution.py:23
  115.2 1.5 collective-permute-start.6
  116.7 1.5 collective-permute-start.22
  118.2 1.8 %collective-permute-done.6 = bf16[2,144,384]{2,1,0:T(8,128)(2,1)S(1)} collective-permute-done((bf16[2,144,384]{2,1,0:T(8,128)(2,1)S(1)}, bf16[2,144,384]{2,1,0:T(8,128)(2,1)S(1)}, u32[]{:S(2)}, u32[]{:S(2)}) %collective-permute-start.6) | collective-permute-done | bytes 221216 | tf_op jit(solution)/shard_map/ppermute | solution.py:23
  120.1 2.9 %collective-permute-start.7 = (bf16[1,144,384]{2,1,0:T(8,128)(2,1)S(1)}, bf16[1,144,384]{2,1,0:T(8,128)(2,1)S(1)}, u32[]{:S(2)}, u32[]{:S(2)}) collective-permute-start(bf16[1,144,384]{2,1,0:T(8,128)(2,1)S(1)} %slice_bitcast_fusion.18), channel_id=1, source_target_pairs={{0,4},{1,5},{2,6},{3,7},{4,0},{5,1},{6,2},{7,3},{8,12},{9,13},{10,... | collective-permute-start | bytes 331784 | tf_op jit(solution)/shard_map/ppermute | solution.py:23
  123.1 4.6 %collective-permute-done.7 = bf16[1,144,384]{2,1,0:T(8,128)(2,1)S(1)} collective-permute-done((bf16[1,144,384]{2,1,0:T(8,128)(2,1)S(1)}, bf16[1,144,384]{2,1,0:T(8,128)(2,1)S(1)}, u32[]{:S(2)}, u32[]{:S(2)}) %collective-permute-start.7) | collective-permute-done | bytes 110624 | tf_op jit(solution)/shard_map/ppermute | solution.py:23
  127.8 5.9 %collective-permute-done.23 = bf16[1,144,1152]{2,1,0:T(8,128)(2,1)S(1)} collective-permute-done((bf16[1,144,1152]{2,1,0:T(8,128)(2,1)S(1)}, bf16[1,144,1152]{2,1,0:T(8,128)(2,1)S(1)}, u32[]{:S(2)}, u32[]{:S(2)}) %collective-permute-start.23) | collective-permute-done | bytes 331808 | tf_op jit(solution)/shard_map/ppermute | solution.py:23
  133.7 0.9 pad_maximum_fusion.1
  134.6 6.2 %collective-permute-start.24 = (bf16[2,144,1152]{2,1,0:T(8,128)(2,1)}, bf16[2,144,1152]{2,1,0:T(8,128)(2,1)}, u32[]{:S(2)}, u32[]{:S(2)}) collective-permute-start(bf16[2,144,1152]{2,1,0:T(8,128)(2,1)} %pad_maximum_fusion.1), channel_id=1, source_target_pairs={{0,8},{8,0},{16,24},{24,16},{1,9},{9,1},{17,25},{25,17},{2,10},{10... | collective-permute-start | bytes 1990664 | tf_op jit(solution)/shard_map/ppermute | solution.py:23
  140.8 0.7 fusion.99
  149.1 1.2 pad_maximum_fusion
  150.4 1.0 bitcast_convert_fusion
  151.3 1.4 maximum_convert_fusion
  (116 shorter events, 8.9 us)
Async XLA Ops:
  0.6 23.0 %copy-start = (bf16[1152,1152]{1,0:T(8,128)(2,1)S(1)}, bf16[1152,1152]{1,0:T(8,128)(2,1)}, u32[]{:S(2)}) copy-start(bf16[1152,1152]{1,0:T(8,128)(2,1)} %param.16) | copy-start | bytes 7962628
  2.8 11.8 %copy-start.13 = (f32[1152]{0:T(1024)S(1)}, f32[1152]{0:T(1024)}, u32[]{:S(2)}) copy-start(f32[1152]{0:T(1024)} %param.14) | copy-start | bytes 13828
  2.8 9.8 %all-to-all-start = ((bf16[2,64,1152]{2,0,1:T(2,128)(2,1)}), bf16[2,64,1152]{2,0,1:T(2,128)(2,1)S(1)}, u32[]{:S(2)}, u32[]{:S(2)}) async-start(bf16[2,64,1152]{2,0,1:T(2,128)(2,1)} %bitcast.228), calls=%async_computation | async-start | bytes 589824 | tf_op jit(solution)/shard_map/all_to_all | solution.py:197
  8.7 4.1 %copy-start.16 = (s32[128]{0:T(128)}, s32[128]{0:T(128)S(1)}, u32[]{:S(2)}) copy-start(s32[128]{0:T(128)S(1)} %convert_reduce_fusion) | copy-start | bytes 1540
  13.8 0.8 copy-start.7
  15.4 4.8 %copy-start.9 = (bf16[128,1152]{1,0:T(8,128)(2,1)}, bf16[128,1152]{1,0:T(8,128)(2,1)S(1)}, u32[]{:S(2)}) copy-start(bf16[128,1152]{1,0:T(8,128)(2,1)S(1)} %fusion.13) | copy-start | bytes 884740
  15.4 4.8 %copy-start.4 = (f32[128,128]{1,0:T(8,128)S(1)}, f32[128,128]{1,0:T(8,128)}, u32[]{:S(2)}) copy-start(f32[128,128]{1,0:T(8,128)} %fusion.61.allowed_ref) | copy-start | bytes 196612
  15.4 8.2 %copy-start.8 = (f32[2,4,16,1152]{3,2,0,1:T(8,128)S(1)}, f32[2,4,16,1152]{3,2,0,1:T(8,128)}, u32[]{:S(2)}) copy-start(f32[2,4,16,1152]{3,2,0,1:T(8,128)} %copy-done.7) | copy-start | bytes 1769476
  23.6 0.8 copy-start.1
  23.6 1.1 copy-start.2
  23.6 1.8 %copy-start.10 = (f32[1152,8]{0,1:T(8,128)S(1)}, f32[1152,8]{0,1:T(8,128)}, u32[]{:S(2)}) copy-start(f32[1152,8]{0,1:T(8,128)} %param.18) | copy-start | bytes 110596
  23.6 1.8 %copy-start.12 = (f32[1152]{0:T(1024)S(1)}, f32[1152]{0:T(1024)}, u32[]{:S(2)}) copy-start(f32[1152]{0:T(1024)} %param.17) | copy-start | bytes 13828
  23.6 2.5 %copy-start.17 = (s32[128]{0:T(128)S(1)}, s32[128]{0:T(128)}, u32[]{:S(2)}) copy-start(s32[128]{0:T(128)} %copy-done.16) | copy-start | bytes 1540
  24.6 0.8 copy-start.5
  25.5 1.6 %copy-start.18 = (f32[128]{0:T(128)}, f32[128]{0:T(128)S(1)}, u32[]{:S(2)}) copy-start(f32[128]{0:T(128)S(1)} %add_rsqrt_fusion.1) | copy-start | bytes 1540
  27.0 9.2 %collective-permute-start = (f32[4,8]{1,0:T(4,128)}, f32[4,8]{1,0:T(4,128)}, u32[]{:S(2)}, u32[]{:S(2)}) collective-permute-start(f32[4,8]{1,0:T(4,128)} %fusion.64), channel_id=1, source_target_pairs={{0,8},{8,0},{16,24},{24,16},{1,9},{9,1},{17,25},{25,17},{2,10},{10... | collective-permute-start | bytes 392 | tf_op jit(solution)/shard_map/ppermute | solution.py:23
  36.2 3.9 %copy-start.11 = (f32[1152,8]{0,1:T(8,128)S(1)}, f32[1152,8]{0,1:T(8,128)}, u32[]{:S(2)}) copy-start(f32[1152,8]{0,1:T(8,128)} %param.18) | copy-start | bytes 110596
  36.2 4.8 %copy-start.6 = (f32[128,1152]{1,0:T(8,128)S(1)}, f32[128,1152]{1,0:T(8,128)}, u32[]{:S(2)}) copy-start(f32[128,1152]{1,0:T(8,128)} %copy-done.5) | copy-start | bytes 1769476
  36.2 6.1 %copy-start.19 = (f32[128]{0:T(128)S(1)}, f32[128]{0:T(128)}, u32[]{:S(2)}) copy-start(f32[128]{0:T(128)} %copy-done.18) | copy-start | bytes 1540
  37.0 2.4 %collective-permute-start.1 = (f32[4,8]{1,0:T(4,128)S(1)}, f32[4,8]{1,0:T(4,128)S(1)}, u32[]{:S(2)}, u32[]{:S(2)}) collective-permute-start(f32[4,8]{1,0:T(4,128)S(1)} %add.220), channel_id=1, source_target_pairs={{0,16},{8,24},{16,0},{24,8},{1,17},{9,25},{17,1},{25,9},{2,18},{10... | collective-permute-start | bytes 392 | tf_op jit(solution)/shard_map/ppermute | solution.py:23
  40.1 3.4 %copy-start.15 = (f32[4,8]{1,0:T(4,128)}, f32[4,8]{1,0:T(4,128)S(1)}, u32[]{:S(2)}) copy-start(f32[4,8]{1,0:T(4,128)S(1)} %add_divide_fusion) | copy-start | bytes 388
  42.6 1.2 copy-start.3
  49.3 7.1 %collective-permute-start.18 = (bf16[8,144,384]{2,1,0:T(8,128)(2,1)S(1)}, bf16[8,144,384]{2,1,0:T(8,128)(2,1)S(1)}, u32[]{:S(2)}, u32[]{:S(2)}) collective-permute-start(bf16[8,144,384]{2,1,0:T(8,128)(2,1)S(1)} %bitcast.274), channel_id=1, source_target_pairs={{0,8},{8,0},{16,24},{24,16},{1,9},{9,1},{17,25},{25,17},{2,10},{10... | collective-permute-start | bytes 2654216 | tf_op jit(solution)/shard_map/ppermute | solution.py:23
  50.9 6.0 %collective-permute-start.16 = (bf16[8,144,384]{2,1,0:T(8,128)(2,1)S(1)}, bf16[8,144,384]{2,1,0:T(8,128)(2,1)S(1)}, u32[]{:S(2)}, u32[]{:S(2)}) collective-permute-start(bf16[8,144,384]{2,1,0:T(8,128)(2,1)S(1)} %bitcast.273), channel_id=1, source_target_pairs={{0,8},{8,0},{16,24},{24,16},{1,9},{9,1},{17,25},{25,17},{2,10},{10... | collective-permute-start | bytes 2654216 | tf_op jit(solution)/shard_map/ppermute | solution.py:23
  52.3 7.0 %collective-permute-start.11 = (bf16[8,144,384]{2,1,0:T(8,128)(2,1)S(1)}, bf16[8,144,384]{2,1,0:T(8,128)(2,1)S(1)}, u32[]{:S(2)}, u32[]{:S(2)}) collective-permute-start(bf16[8,144,384]{2,1,0:T(8,128)(2,1)S(1)} %bitcast.272), channel_id=1, source_target_pairs={{0,8},{8,0},{16,24},{24,16},{1,9},{9,1},{17,25},{25,17},{2,10},{10... | collective-permute-start | bytes 2654216 | tf_op jit(solution)/shard_map/ppermute | solution.py:23
  54.2 5.5 %collective-permute-start.8 = (bf16[8,144,384]{2,1,0:T(8,128)(2,1)S(1)}, bf16[8,144,384]{2,1,0:T(8,128)(2,1)S(1)}, u32[]{:S(2)}, u32[]{:S(2)}) collective-permute-start(bf16[8,144,384]{2,1,0:T(8,128)(2,1)S(1)} %bitcast.271), channel_id=1, source_target_pairs={{0,8},{8,0},{16,24},{24,16},{1,9},{9,1},{17,25},{25,17},{2,10},{10... | collective-permute-start | bytes 2654216 | tf_op jit(solution)/shard_map/ppermute | solution.py:23
  54.7 6.7 %collective-permute-start.3 = (bf16[8,144,384]{2,1,0:T(8,128)(2,1)S(1)}, bf16[8,144,384]{2,1,0:T(8,128)(2,1)S(1)}, u32[]{:S(2)}, u32[]{:S(2)}) collective-permute-start(bf16[8,144,384]{2,1,0:T(8,128)(2,1)S(1)} %bitcast.270), channel_id=1, source_target_pairs={{0,8},{8,0},{16,24},{24,16},{1,9},{9,1},{17,25},{25,17},{2,10},{10... | collective-permute-start | bytes 2654216 | tf_op jit(solution)/shard_map/ppermute | solution.py:23
  56.5 48.0 %collective-permute-start.2 = (bf16[8,144,384]{2,1,0:T(8,128)(2,1)S(1)}, bf16[8,144,384]{2,1,0:T(8,128)(2,1)S(1)}, u32[]{:S(2)}, u32[]{:S(2)}) collective-permute-start(bf16[8,144,384]{2,1,0:T(8,128)(2,1)S(1)} %bitcast.269), channel_id=1, source_target_pairs={{0,8},{8,0},{16,24},{24,16},{1,9},{9,1},{17,25},{25,17},{2,10},{10... | collective-permute-start | bytes 2654216 | tf_op jit(solution)/shard_map/ppermute | solution.py:23
  56.9 12.1 %collective-permute-start.19 = (bf16[4,144,384]{2,1,0:T(8,128)(2,1)S(1)}, bf16[4,144,384]{2,1,0:T(8,128)(2,1)S(1)}, u32[]{:S(2)}, u32[]{:S(2)}) collective-permute-start(bf16[4,144,384]{2,1,0:T(8,128)(2,1)S(1)} %bitcast.276), channel_id=1, source_target_pairs={{0,2},{1,3},{2,0},{3,1},{4,6},{5,7},{6,4},{7,5},{8,10},{9,11},{10,... | collective-permute-start | bytes 1327112 | tf_op jit(solution)/shard_map/ppermute | solution.py:23
  59.3 27.2 %collective-permute-start.17 = (bf16[4,144,384]{2,1,0:T(8,128)(2,1)S(1)}, bf16[4,144,384]{2,1,0:T(8,128)(2,1)S(1)}, u32[]{:S(2)}, u32[]{:S(2)}) collective-permute-start(bf16[4,144,384]{2,1,0:T(8,128)(2,1)S(1)} %bitcast.275), channel_id=1, source_target_pairs={{0,2},{1,3},{2,0},{3,1},{4,6},{5,7},{6,4},{7,5},{8,10},{9,11},{10,... | collective-permute-start | bytes 1327112 | tf_op jit(solution)/shard_map/ppermute | solution.py:23
  59.7 11.0 %collective-permute-start.12 = (bf16[4,144,384]{2,1,0:T(8,128)(2,1)S(1)}, bf16[4,144,384]{2,1,0:T(8,128)(2,1)S(1)}, u32[]{:S(2)}, u32[]{:S(2)}) collective-permute-start(bf16[4,144,384]{2,1,0:T(8,128)(2,1)S(1)} %slice_bitcast_fusion), channel_id=1, source_target_pairs={{0,1},{1,0},{2,3},{3,2},{4,5},{5,4},{6,7},{7,6},{8,9},{9,8},{10,11... | collective-permute-start | bytes 1327112 | tf_op jit(solution)/shard_map/ppermute | solution.py:23
  61.4 18.7 %collective-permute-start.9 = (bf16[4,144,384]{2,1,0:T(8,128)(2,1)S(1)}, bf16[4,144,384]{2,1,0:T(8,128)(2,1)S(1)}, u32[]{:S(2)}, u32[]{:S(2)}) collective-permute-start(bf16[4,144,384]{2,1,0:T(8,128)(2,1)S(1)} %slice_bitcast_fusion.2), channel_id=1, source_target_pairs={{0,1},{1,0},{2,3},{3,2},{4,5},{5,4},{6,7},{7,6},{8,9},{9,8},{10,11... | collective-permute-start | bytes 1327112 | tf_op jit(solution)/shard_map/ppermute | solution.py:23
  69.0 35.4 %collective-permute-start.4 = (bf16[8,144,384]{2,1,0:T(8,128)(2,1)S(1)}, bf16[8,144,384]{2,1,0:T(8,128)(2,1)S(1)}, u32[]{:S(2)}, u32[]{:S(2)}) collective-permute-start(bf16[8,144,384]{2,1,0:T(8,128)(2,1)S(1)} %fusion.4), channel_id=1, source_target_pairs={{0,16},{8,24},{16,0},{24,8},{1,17},{9,25},{17,1},{25,9},{2,18},{10... | collective-permute-start | bytes 2654216 | tf_op jit(solution)/shard_map/ppermute | solution.py:23
  70.7 27.4 %collective-permute-start.20 = (bf16[4,144,384]{2,1,0:T(8,128)(2,1)S(1)}, bf16[4,144,384]{2,1,0:T(8,128)(2,1)S(1)}, u32[]{:S(2)}, u32[]{:S(2)}) collective-permute-start(bf16[4,144,384]{2,1,0:T(8,128)(2,1)S(1)} %fusion.6), channel_id=1, source_target_pairs={{0,16},{8,24},{16,0},{24,8},{1,17},{9,25},{17,1},{25,9},{2,18},{10... | collective-permute-start | bytes 1327112 | tf_op jit(solution)/shard_map/ppermute | solution.py:23
  80.2 5.3 %collective-permute-start.13 = (bf16[2,144,384]{2,1,0:T(8,128)(2,1)S(1)}, bf16[2,144,384]{2,1,0:T(8,128)(2,1)S(1)}, u32[]{:S(2)}, u32[]{:S(2)}) collective-permute-start(bf16[2,144,384]{2,1,0:T(8,128)(2,1)S(1)} %slice_bitcast_fusion.8), channel_id=1, source_target_pairs={{0,2},{1,3},{2,0},{3,1},{4,6},{5,7},{6,4},{7,5},{8,10},{9,11},{10,... | collective-permute-start | bytes 663560 | tf_op jit(solution)/shard_map/ppermute | solution.py:23
  85.4 13.4 %collective-permute-start.10 = (bf16[2,144,384]{2,1,0:T(8,128)(2,1)S(1)}, bf16[2,144,384]{2,1,0:T(8,128)(2,1)S(1)}, u32[]{:S(2)}, u32[]{:S(2)}) collective-permute-start(bf16[2,144,384]{2,1,0:T(8,128)(2,1)S(1)} %slice_bitcast_fusion.10), channel_id=1, source_target_pairs={{0,2},{1,3},{2,0},{3,1},{4,6},{5,7},{6,4},{7,5},{8,10},{9,11},{10,... | collective-permute-start | bytes 663560 | tf_op jit(solution)/shard_map/ppermute | solution.py:23
  86.4 16.3 %collective-permute-start.14 = (bf16[2,144,384]{2,1,0:T(8,128)(2,1)S(1)}, bf16[2,144,384]{2,1,0:T(8,128)(2,1)S(1)}, u32[]{:S(2)}, u32[]{:S(2)}) collective-permute-start(bf16[2,144,384]{2,1,0:T(8,128)(2,1)S(1)} %fusion.19), channel_id=1, source_target_pairs={{0,16},{8,24},{16,0},{24,8},{1,17},{9,25},{17,1},{25,9},{2,18},{10... | collective-permute-start | bytes 663560 | tf_op jit(solution)/shard_map/ppermute | solution.py:23
  98.3 10.4 %collective-permute-start.21 = (bf16[2,144,384]{2,1,0:T(8,128)(2,1)S(1)}, bf16[2,144,384]{2,1,0:T(8,128)(2,1)S(1)}, u32[]{:S(2)}, u32[]{:S(2)}) collective-permute-start(bf16[2,144,384]{2,1,0:T(8,128)(2,1)S(1)} %slice_bitcast_fusion.6), channel_id=1, source_target_pairs={{0,1},{1,0},{2,3},{3,2},{4,5},{5,4},{6,7},{7,6},{8,9},{9,8},{10,11... | collective-permute-start | bytes 663560 | tf_op jit(solution)/shard_map/ppermute | solution.py:23
  102.9 5.7 %collective-permute-start.15 = (bf16[1,144,384]{2,1,0:T(8,128)(2,1)S(1)}, bf16[1,144,384]{2,1,0:T(8,128)(2,1)S(1)}, u32[]{:S(2)}, u32[]{:S(2)}) collective-permute-start(bf16[1,144,384]{2,1,0:T(8,128)(2,1)S(1)} %slice_bitcast_fusion.16), channel_id=1, source_target_pairs={{0,4},{1,5},{2,6},{3,7},{4,0},{5,1},{6,2},{7,3},{8,12},{9,13},{10,... | collective-permute-start | bytes 331784 | tf_op jit(solution)/shard_map/ppermute | solution.py:23
  104.9 10.2 %collective-permute-start.5 = (bf16[4,144,384]{2,1,0:T(8,128)(2,1)S(1)}, bf16[4,144,384]{2,1,0:T(8,128)(2,1)S(1)}, u32[]{:S(2)}, u32[]{:S(2)}) collective-permute-start(bf16[4,144,384]{2,1,0:T(8,128)(2,1)S(1)} %slice_bitcast_fusion.4), channel_id=1, source_target_pairs={{0,1},{1,0},{2,3},{3,2},{4,5},{5,4},{6,7},{7,6},{8,9},{9,8},{10,11... | collective-permute-start | bytes 1327112 | tf_op jit(solution)/shard_map/ppermute | solution.py:23
  115.2 4.8 %collective-permute-start.6 = (bf16[2,144,384]{2,1,0:T(8,128)(2,1)S(1)}, bf16[2,144,384]{2,1,0:T(8,128)(2,1)S(1)}, u32[]{:S(2)}, u32[]{:S(2)}) collective-permute-start(bf16[2,144,384]{2,1,0:T(8,128)(2,1)S(1)} %slice_bitcast_fusion.12), channel_id=1, source_target_pairs={{0,2},{1,3},{2,0},{3,1},{4,6},{5,7},{6,4},{7,5},{8,10},{9,11},{10,... | collective-permute-start | bytes 663560 | tf_op jit(solution)/shard_map/ppermute | solution.py:23
  116.7 24.1 %copy-start.14 = (s32[4]{0:T(128)S(1)}, s32[4]{0:T(128)}, u32[]{:S(2)}) copy-start(s32[4]{0:T(128)} %constant.114.clone) | copy-start | bytes 52
  116.7 6.3 %collective-permute-start.22 = (bf16[1,144,384]{2,1,0:T(8,128)(2,1)S(1)}, bf16[1,144,384]{2,1,0:T(8,128)(2,1)S(1)}, u32[]{:S(2)}, u32[]{:S(2)}) collective-permute-start(bf16[1,144,384]{2,1,0:T(8,128)(2,1)S(1)} %slice_bitcast_fusion.14), channel_id=1, source_target_pairs={{0,4},{1,5},{2,6},{3,7},{4,0},{5,1},{6,2},{7,3},{8,12},{9,13},{10,... | collective-permute-start | bytes 331784 | tf_op jit(solution)/shard_map/ppermute | solution.py:23
  120.1 7.5 %collective-permute-start.7 = (bf16[1,144,384]{2,1,0:T(8,128)(2,1)S(1)}, bf16[1,144,384]{2,1,0:T(8,128)(2,1)S(1)}, u32[]{:S(2)}, u32[]{:S(2)}) collective-permute-start(bf16[1,144,384]{2,1,0:T(8,128)(2,1)S(1)} %slice_bitcast_fusion.18), channel_id=1, source_target_pairs={{0,4},{1,5},{2,6},{3,7},{4,0},{5,1},{6,2},{7,3},{8,12},{9,13},{10,... | collective-permute-start | bytes 331784 | tf_op jit(solution)/shard_map/ppermute | solution.py:23
  127.7 6.0 %collective-permute-start.23 = (bf16[1,144,1152]{2,1,0:T(8,128)(2,1)S(1)}, bf16[1,144,1152]{2,1,0:T(8,128)(2,1)S(1)}, u32[]{:S(2)}, u32[]{:S(2)}) collective-permute-start(bf16[1,144,1152]{2,1,0:T(8,128)(2,1)S(1)} %maximum_bitcast_fusion), channel_id=1, source_target_pairs={{0,16},{8,24},{16,0},{24,8},{1,17},{9,25},{17,1},{25,9},{2,18},{10... | collective-permute-start | bytes 995336 | tf_op jit(solution)/shard_map/ppermute | solution.py:23
  134.6 14.5 %collective-permute-start.24 = (bf16[2,144,1152]{2,1,0:T(8,128)(2,1)}, bf16[2,144,1152]{2,1,0:T(8,128)(2,1)}, u32[]{:S(2)}, u32[]{:S(2)}) collective-permute-start(bf16[2,144,1152]{2,1,0:T(8,128)(2,1)} %pad_maximum_fusion.1), channel_id=1, source_target_pairs={{0,8},{8,0},{16,24},{24,16},{1,9},{9,1},{17,25},{25,17},{2,10},{10... | collective-permute-start | bytes 1990664 | tf_op jit(solution)/shard_map/ppermute | solution.py:23
where the time goes:
time: 153 us
  waiting for transfers between devices  61.4 us (40%)
  starting transfers between devices  29.8 us (19%)
  other arithmetic  15.1 us (10%)
  matrix products  15 us (10%)
  local copies, waits for them, and re-layouts  14.1 us (9%)
  between operations  8.86 us (6%)
  Pallas kernels  8.47 us (6%)
    ppermute x25, waiting for transfers between devices, swapped(): return lax.ppermute(block, axis, route)  59.5 us
    ppermute x25, starting transfers between devices, swapped(): return lax.ppermute(block, axis, route)  25.4 us
    pallas_call x1, Pallas kernels, attend_grad(): pl.pallas_call(backward_kernel, out_shape=jax.ShapeDtypeStruct(projected....  5.1 us
    dot_general x12, matrix products, product(): full = jnp.dot(left, right, preferred_element_type=jnp.float32)  4.95 us
    dot_general x1, matrix products, on_device(): jnp.dot(normed, w_qkv, preferred_element_type=jnp.float32)  4.74 us
    gather x2, local copies, waits for them, and re-layouts, relative_rows(): blocks = jnp.take(values.T.reshape(n_dp, rows, count), order, axis=0)  4.5 us
    all_to_all x1, starting transfers between devices, on_device(): lax.all_to_all(tokens[0], 'tm', split_axis=1, concat_axis=0, tiled=True)  4.42 us
    unnamed x41, local copies, waits for them, and re-layouts  4.09 us
  transfers between devices with their start and end apart: 26, of which 13 were waited for; matrix products, arithmetic and copies ran while one was open for 14% of the time, Pallas kernels for 0%

commit v1 on v0

--- a/solution.py
+++ b/solution.py
@@ -125,13 +125,11 @@
     rows = width // n_dp
     columns = grads.shape[1] // n_tm
     first_out = n_tm * 3 // 4
-    order = me_dp ^ jnp.arange(n_dp, dtype=jnp.int32)
-
-    def relative_rows(values):
-        blocks = jnp.take(values.T.reshape(n_dp, rows, count), order, axis=0)
-        return blocks.reshape(width, count)
-
-    left_qkv, left_out = relative_rows(normed), relative_rows(attended)
+    row = jnp.arange(width, dtype=jnp.int32)
+    source = (row // rows ^ me_dp) * rows + row % rows
+    places = (source[:, None] == row[None, :]).astype(jnp.bfloat16)
+    left_qkv = dot_nt(places, normed).astype(jnp.bfloat16)
+    left_out = dot_nt(places, attended).astype(jnp.bfloat16)
     pieces = 3
     piece = columns // pieces
     bits_tm, bits_dp = n_tm.bit_length() - 1, n_dp.bit_length() - 1
@@ -151,39 +149,46 @@
     for part in range(pieces):
         for number in sorted(range(n_tm), key=lambda r: (1 - (r & 1), r)):
             held[part][number] = product(part, number)
+    def halves(part, at):
+        axis, bit = steps[part][at]
+        blocks = held[part]
+        if axis == "tm":
+            kept = {r: blocks[r] for r in blocks if not (r >> bit) & 1}
+            return kept, {r: blocks[r ^ (1 << bit)] for r in kept}
+        done = sum(1 for a, b in steps[part][:at] if a == "dp" and b < bit)
+        size = 1 << (bit - done)
+        kept, going = {}, {}
+        for r in blocks:
+            pair = blocks[r].reshape(-1, 2, size, rows, piece)
+            kept[r] = pair[:, 0].reshape(-1, rows, piece)
+            going[r] = pair[:, 1].reshape(-1, rows, piece)
+        return kept, going
+
     for at in range(len(steps[0])):
+        split = [halves(part, at) for part in range(pieces)]
+        if at == 0:
+            sends = [[going[r] for r in going] for _, going in split]
+        else:
+            sends = [[jnp.concatenate([going[r] for r in going], axis=0)] for _, going in split]
+            sends = lax.optimization_barrier(sends)
         for part in range(pieces):
-            axis, bit = steps[part][at]
-            blocks = held[part]
-            if axis == "tm":
-                going = [r for r in blocks if (r >> bit) & 1]
-                for r in going:
-                    other = swapped(blocks.pop(r), "tm", bit)
-                    kept = r ^ (1 << bit)
-                    total = blocks[kept].astype(jnp.float32) + other.astype(jnp.float32)
-                    blocks[kept] = total.astype(jnp.bfloat16)
-            else:
-                for r in blocks:
-                    done = sum(1 for a, b in steps[part][:at] if a == "dp" and b < bit)
-                    size = 1 << (bit - done)
-                    rank = blocks[r].shape[0] // (2 * size)
-                    pair = blocks[r].reshape(rank, 2, size, rows, piece)
-                    kept = pair[:, 0].reshape(rank * size, rows, piece)
-                    going = pair[:, 1].reshape(rank * size, rows, piece)
-                    other = swapped(going, "dp", bit)
-                    total = kept.astype(jnp.float32) + other.astype(jnp.float32)
-                    blocks[r] = total.astype(jnp.bfloat16)
+            kept = split[part][0]
+            came = [swapped(block, *steps[part][at]) for block in sends[part]]
+            if len(came) < len(kept):
+                came = jnp.split(came[0], len(kept), axis=0)
+            for r, other in zip(kept, came):
+                total = kept[r].astype(jnp.float32) + other.astype(jnp.float32)
+                kept[r] = total.astype(jnp.bfloat16)
+            held[part] = kept
     mine = jnp.concatenate([held[part][0][0] for part in range(pieces)], axis=1)
-    gathered = mine[None]
-    for bit in reversed(range(bits_tm)):
-        gathered = jnp.concatenate([gathered, swapped(gathered, "tm", bit)], axis=0)
-    place = []
-    for number in range(n_tm):
-        place.append(sum(((number >> b) & 1) << (bits_tm - 1 - b) for b in range(bits_tm)))
-    place = jnp.array(place, dtype=jnp.int32)
-    whole = []
-    for block in range(n_tm):
-        whole.append(lax.dynamic_index_in_dim(gathered, place[me_tm ^ block], 0, keepdims=False))
+    gathered = {0: mine}
+    for bit in list(range(1, bits_tm))[::-1] + [0]:
+        for r in list(gathered):
+            gathered[r ^ (1 << bit)] = swapped(gathered[r], "tm", bit)
+    whole = [gathered[r] for r in range(n_tm)]
+    for bit in range(bits_tm):
+        odd = (me_tm >> bit) & 1 == 1
+        whole = [jnp.where(odd, whole[r ^ (1 << bit)], whole[r]) for r in range(n_tm)]
     qkv = jnp.concatenate(whole[:first_out], axis=1).astype(jnp.float32)
     out = jnp.concatenate(whole[first_out:], axis=1).astype(jnp.float32)
     return qkv, out

time: 153 us -> 126 us (0.82)
  waiting for transfers between devices: 61.4 us -> 52.5 us
  local copies, waits for them, and re-layouts: 14.1 us -> 5.6 us
  between operations: 8.86 us -> 1.34 us
  starting transfers between devices: 29.8 us -> 28.1 us
    ppermute x25 -> x23, waiting for transfers between devices: 59.5 us -> 48.9 us  [swapped(): return lax.ppermute(block, axis, route)]
    gather x2 -> x0, local copies, waits for them, and re-layouts: 4.5 us -> none  [relative_rows(): blocks = jnp.take(values.T.reshape(n_dp, rows, count), order, axis=0)]
    transpose x2 -> x0, local copies, waits for them, and re-layouts: 3.69 us -> none  [relative_rows(): blocks = jnp.take(values.T.reshape(n_dp, rows, count), order, axis=0)]
    dot_general x1 -> x3, matrix products: 0.91 us -> 3.03 us  [dot_nt(): lax.dot_general(left, right, (((1,), (1,)), ((), ())), preferred_element_...]
    convert_element_type x12 -> x11, other arithmetic: 2.34 us -> 4.4 us  [summed_blocks(): kept[r] = total.astype(jnp.bfloat16)]
    ppermute x25 -> x23, starting transfers between devices: 25.4 us -> 23.7 us  [swapped(): return lax.ppermute(block, axis, route)]
    all_to_all x1, waiting for transfers between devices: 1.92 us -> 3.56 us  [on_device(): lax.all_to_all(tokens[0], 'tm', split_axis=1, concat_axis=0, tiled=True)]
    unnamed x41 -> x39, local copies, waits for them, and re-layouts: 4.09 us -> 3.41 us
  transfers between devices with their start and end apart: 26 -> 24, of which waited for: 13 -> 11; matrix products, arithmetic and copies ran while one was open for 14% -> 13% of each run, Pallas kernels for 0% -> 0%
where the time goes in v1:
time: 126 us
  waiting for transfers between devices  52.5 us (42%)
  starting transfers between devices  28.1 us (22%)
  matrix products  16.2 us (13%)
  other arithmetic  13.6 us (11%)
  Pallas kernels  8.47 us (7%)
  local copies, waits for them, and re-layouts  5.6 us (4%)
  between operations  1.34 us (1%)
    ppermute x23, waiting for transfers between devices, swapped(): return lax.ppermute(block, axis, route)  48.9 us
    ppermute x23, starting transfers between devices, swapped(): return lax.ppermute(block, axis, route)  23.7 us
    dot_general x12, matrix products, product(): full = jnp.dot(left, right, preferred_element_type=jnp.float32)  6.07 us
    pallas_call x1, Pallas kernels, attend_grad(): pl.pallas_call(backward_kernel, out_shape=jax.ShapeDtypeStruct(projected....  5.1 us
    dot_general x1, matrix products, on_device(): jnp.dot(normed, w_qkv, preferred_element_type=jnp.float32)  4.62 us
    all_to_all x1, starting transfers between devices, on_device(): lax.all_to_all(tokens[0], 'tm', split_axis=1, concat_axis=0, tiled=True)  4.42 us
    convert_element_type x11, other arithmetic, summed_blocks(): kept[r] = total.astype(jnp.bfloat16)  4.4 us
    all_to_all x1, waiting for transfers between devices, on_device(): lax.all_to_all(tokens[0], 'tm', split_axis=1, concat_axis=0, tiled=True)  3.56 us
  transfers between devices with their start and end apart: 24, of which 11 were waited for; matrix products, arithmetic and copies ran while one was open for 13% of the time, Pallas kernels for 0%

profile of v1, /device:TPU:1, one launch (start us, length us, event | category | flops | bytes accessed | tf_op | source)
XLA Modules:
  0.0 125.8 jit_solution(17242435117115525027)
XLA Ops:
  0.6 2.1 %copy.100 = bf16[1,2,64,1152]{3,1,2,0:T(2,128)(2,1)} copy(bf16[1,2,64,1152]{3,2,1,0:T(8,128)(2,1)} %param.8) | data formatting | bytes 589824 | tf_op args[0]
  2.8 4.4 %all-to-all-start = ((bf16[2,64,1152]{2,0,1:T(2,128)(2,1)}), bf16[2,64,1152]{2,0,1:T(2,128)(2,1)S(1)}, u32[]{:S(2)}, u32[]{:S(2)}) async-start(bf16[2,64,1152]{2,0,1:T(2,128)(2,1)} %bitcast.209), calls=%async_computation | async-start | bytes 589824 | tf_op jit(solution)/shard_map/all_to_all | solution.py:202
  7.2 0.8 reduce-window.8
  8.3 0.7 multiply_bitcast_fusion
  9.0 3.6 %all-to-all-done = bf16[2,64,1152]{2,0,1:T(2,128)(2,1)S(1)} async-done(((bf16[2,64,1152]{2,0,1:T(2,128)(2,1)}), bf16[2,64,1152]{2,0,1:T(2,128)(2,1)S(1)}, u32[]{:S(2)}, u32[]{:S(2)}) %all-to-all-start) | async-done | bytes 294944 | tf_op jit(solution)/shard_map/all_to_all | solution.py:202
  13.5 4.6 %convolution_convert_fusion.projected_ref = bf16[128,3456]{1,0:T(8,128)(2,1)S(1)} fusion(bf16[128,1152]{1,0:T(8,128)(2,1)S(1)} %fusion.19, bf16[1152,3456]{1,0:T(8,128)(2,1)} %param.12), kind=kOutput, calls=%fused_computation.3 | convolution fusion | flops 1019658240 | bytes 9142272 | tf_op jit(solution)/shard_map/dot_general | solution.py:220
  18.1 3.4 %shard_map.103 = (bf16[128,1152]{1,0:T(8,128)(2,1)S(1)}, f32[16,128,128]{2,1,0:T(8,128)S(1)}) custom-call(bf16[128,3456]{1,0:T(8,128)(2,1)S(1)} %convolution_convert_fusion.projected_ref, f32[128,128]{1,0:T(8,128)S(1)} %fusion.67.allowed_ref), custom_call_target="tpu_custom_call" | custom-call | tf_op jit(solution)/shard_map/pallas_call | solution.py:97
  21.6 0.7 fusion.115
  22.5 0.7 fusion.22
  23.5 1.1 collective-permute-start
  24.5 1.0 fusion.5
  25.8 1.1 broadcast_select_fusion.9
  26.8 1.3 %collective-permute-done.1 = f32[4,8]{1,0:T(4,128)S(1)} collective-permute-done((f32[4,8]{1,0:T(4,128)S(1)}, f32[4,8]{1,0:T(4,128)S(1)}, u32[]{:S(2)}, u32[]{:S(2)}) %collective-permute-start.1) | collective-permute-done | bytes 160 | tf_op jit(solution)/shard_map/ppermute | solution.py:23
  28.4 0.6 fusion.112
  29.3 0.9 convolution_convert_fusion.13.grad_ref
  30.2 5.1 %shard_map.104 = bf16[128,3456]{1,0:T(8,128)(2,1)S(1)} custom-call(bf16[128,3456]{1,0:T(8,128)(2,1)S(1)} %convolution_convert_fusion.projected_ref, f32[16,128,128]{2,1,0:T(8,128)S(1)} %get-tuple-element.18.weights_ref, bf16[128,1152]{1,0:T(8,128)(2,1)S(1)} %convolution_convert_fusion.13.grad_ref), custom_call_target="tpu_custom_call" | custom-call | tf_op jit(solution)/shard_map/pallas_call | solution.py:111
  35.3 0.4 convolution_convert_fusion.3
  35.7 1.2 collective-permute-start.6
  37.0 0.4 convolution_convert_fusion.1
  37.4 0.6 convolution_convert_fusion.7
  38.0 0.5 collective-permute-start.4
  38.6 0.4 convolution_convert_fusion.4
  39.0 0.4 convolution_convert_fusion.8
  39.4 0.4 convolution_convert_fusion.5
  39.9 0.4 convolution_convert_fusion.2
  40.3 0.4 convolution_convert_fusion.6
  40.7 0.4 convolution_convert_fusion.9
  41.1 0.5 collective-permute-start.3
  41.7 0.4 convolution_convert_fusion.10
  42.3 0.9 fusion.113
  43.5 0.9 fusion.114
  44.3 1.0 pad_maximum_fusion.1
  45.9 0.6 copy-done.3
  46.6 1.1 pad_maximum_fusion
  47.7 1.2 fusion.10
  48.9 1.8 %collective-permute-start.9 = (bf16[8,144,384]{2,1,0:T(8,128)(2,1)}, bf16[8,144,384]{2,1,0:T(8,128)(2,1)}, u32[]{:S(2)}, u32[]{:S(2)}) collective-permute-start(bf16[8,144,384]{2,1,0:T(8,128)(2,1)} %pad_maximum_fusion), channel_id=1, source_target_pairs={{0,1},{1,0},{2,3},{3,2},{4,5},{5,4},{6,7},{7,6},{8,9},{9,8},{10,11... | collective-permute-start | bytes 2654216 | tf_op jit(solution)/shard_map/ppermute | solution.py:23
  50.7 1.5 %convolution_convert_fusion.11 = bf16[1152,384]{1,0:T(8,128)(2,1)S(1)} fusion(bf16[1152,128]{1,0:T(8,128)(2,1)} %copy-done.9, s32[]{:T(128)S(6)} %select_n.178, bf16[128,3456]{1,0:T(8,128)(2,1)S(1)} %shard_map.104, bf16[128,1152]{1,0:T(8,128)(2,1)} %copy-done.1), kind=kOutput, calls=%fused_computation.26 | convolution fusion | flops 113885184 | bytes 2359300 | tf_op jit(solution)/shard_map/dot_general | solution.py:144
  52.2 0.4 collective-permute-start.2
  52.7 0.4 convolution_convert_fusion.12
  53.1 1.4 %collective-permute-start.10 = (bf16[8,144,384]{2,1,0:T(8,128)(2,1)S(1)}, bf16[8,144,384]{2,1,0:T(8,128)(2,1)S(1)}, u32[]{:S(2)}, u32[]{:S(2)}) collective-permute-start(bf16[8,144,384]{2,1,0:T(8,128)(2,1)S(1)} %copy-done.12), channel_id=1, source_target_pairs={{0,2},{1,3},{2,0},{3,1},{4,6},{5,7},{6,4},{7,5},{8,10},{9,11},{10,... | collective-permute-start | bytes 2654216 | tf_op jit(solution)/shard_map/ppermute | solution.py:23
  54.5 16.5 %collective-permute-done.9 = bf16[8,144,384]{2,1,0:T(8,128)(2,1)} collective-permute-done((bf16[8,144,384]{2,1,0:T(8,128)(2,1)}, bf16[8,144,384]{2,1,0:T(8,128)(2,1)}, u32[]{:S(2)}, u32[]{:S(2)}) %collective-permute-start.9) | collective-permute-done | bytes 884768 | tf_op jit(solution)/shard_map/ppermute | solution.py:23
  71.0 1.4 %fusion.15 = (bf16[4,144,384]{2,1,0:T(8,128)(2,1)S(1)}, bf16[4,144,384]{2,1,0:T(8,128)(2,1)S(1)}) fusion(bf16[8,144,384]{2,1,0:T(8,128)(2,1)} %collective-permute-done.9, bf16[4,2,1,144,384]{4,3,1,0,2:T(8,128)(2,1)S(1)} %bitcast.222, bf16[4,2,1,144,384]{4,3,1,0,2:T(8,128)(2,1)S(1)} %bitcast.224), kind=kLoop, calls=%fused_computation.70 | loop fusion | flops 1769472 | bytes 2654208 | tf_op jit(solution)/shard_map/convert_element_type | solution.py:181
  72.5 1.1 collective-permute-done.8
  73.7 0.3 add_convert_fusion
  74.1 0.6 copy-done.11
  75.0 0.7 collective-permute-start.13
  75.7 1.4 %collective-permute-start.12 = (bf16[4,144,384]{2,1,0:T(8,128)(2,1)S(1)}, bf16[4,144,384]{2,1,0:T(8,128)(2,1)S(1)}, u32[]{:S(2)}, u32[]{:S(2)}) collective-permute-start(bf16[4,144,384]{2,1,0:T(8,128)(2,1)S(1)} %pad_maximum_fusion.2), channel_id=1, source_target_pairs={{0,2},{1,3},{2,0},{3,1},{4,6},{5,7},{6,4},{7,5},{8,10},{9,11},{10,... | collective-permute-start | bytes 1327112 | tf_op jit(solution)/shard_map/ppermute | solution.py:23
  77.1 8.5 %collective-permute-done.11 = bf16[4,144,384]{2,1,0:T(8,128)(2,1)S(1)} collective-permute-done((bf16[4,144,384]{2,1,0:T(8,128)(2,1)S(1)}, bf16[4,144,384]{2,1,0:T(8,128)(2,1)S(1)}, u32[]{:S(2)}, u32[]{:S(2)}) %collective-permute-start.11) | collective-permute-done | bytes 442400 | tf_op jit(solution)/shard_map/ppermute | solution.py:23
  86.1 1.1 collective-permute-start.16
  87.2 0.9 collective-permute-start.15
  88.1 1.3 %collective-permute-start.14 = (bf16[2,144,384]{2,1,0:T(8,128)(2,1)S(1)}, bf16[2,144,384]{2,1,0:T(8,128)(2,1)S(1)}, u32[]{:S(2)}, u32[]{:S(2)}) collective-permute-start(bf16[2,144,384]{2,1,0:T(8,128)(2,1)S(1)} %slice_bitcast_fusion.10), channel_id=1, source_target_pairs={{0,2},{1,3},{2,0},{3,1},{4,6},{5,7},{6,4},{7,5},{8,10},{9,11},{10,... | collective-permute-start | bytes 663560 | tf_op jit(solution)/shard_map/ppermute | solution.py:23
  89.4 1.6 %collective-permute-done.16 = bf16[2,144,384]{2,1,0:T(8,128)(2,1)S(1)} collective-permute-done((bf16[2,144,384]{2,1,0:T(8,128)(2,1)S(1)}, bf16[2,144,384]{2,1,0:T(8,128)(2,1)S(1)}, u32[]{:S(2)}, u32[]{:S(2)}) %collective-permute-start.16) | collective-permute-done | bytes 221216 | tf_op jit(solution)/shard_map/ppermute | solution.py:23
  91.0 1.3 %collective-permute-done.15 = bf16[2,144,384]{2,1,0:T(8,128)(2,1)S(1)} collective-permute-done((bf16[2,144,384]{2,1,0:T(8,128)(2,1)S(1)}, bf16[2,144,384]{2,1,0:T(8,128)(2,1)S(1)}, u32[]{:S(2)}, u32[]{:S(2)}) %collective-permute-start.15) | collective-permute-done | bytes 221216 | tf_op jit(solution)/shard_map/ppermute | solution.py:23
  92.4 0.8 collective-permute-done.14
  93.2 2.4 %collective-permute-start.17 = (bf16[1,144,384]{2,1,0:T(8,128)(2,1)S(1)}, bf16[1,144,384]{2,1,0:T(8,128)(2,1)S(1)}, u32[]{:S(2)}, u32[]{:S(2)}) collective-permute-start(bf16[1,144,384]{2,1,0:T(8,128)(2,1)S(1)} %slice_bitcast_fusion.18), channel_id=1, source_target_pairs={{0,4},{1,5},{2,6},{3,7},{4,0},{5,1},{6,2},{7,3},{8,12},{9,13},{10,... | collective-permute-start | bytes 331784 | tf_op jit(solution)/shard_map/ppermute | solution.py:23
  95.7 2.3 %collective-permute-start.19 = (bf16[1,144,384]{2,1,0:T(8,128)(2,1)S(1)}, bf16[1,144,384]{2,1,0:T(8,128)(2,1)S(1)}, u32[]{:S(2)}, u32[]{:S(2)}) collective-permute-start(bf16[1,144,384]{2,1,0:T(8,128)(2,1)S(1)} %slice_bitcast_fusion.16), channel_id=1, source_target_pairs={{0,4},{1,5},{2,6},{3,7},{4,0},{5,1},{6,2},{7,3},{8,12},{9,13},{10,... | collective-permute-start | bytes 331784 | tf_op jit(solution)/shard_map/ppermute | solution.py:23
  98.0 11.9 %collective-permute-done.19 = bf16[1,144,384]{2,1,0:T(8,128)(2,1)S(1)} collective-permute-done((bf16[1,144,384]{2,1,0:T(8,128)(2,1)S(1)}, bf16[1,144,384]{2,1,0:T(8,128)(2,1)S(1)}, u32[]{:S(2)}, u32[]{:S(2)}) %collective-permute-start.19) | collective-permute-done | bytes 110624 | tf_op jit(solution)/shard_map/ppermute | solution.py:23
  110.0 0.6 collective-permute-start.20
  110.7 2.4 %collective-permute-start.22 = (bf16[144,1152]{1,0:T(8,128)(2,1)S(1)}, bf16[144,1152]{1,0:T(8,128)(2,1)}, u32[]{:S(2)}, u32[]{:S(2)}) collective-permute-start(bf16[144,1152]{1,0:T(8,128)(2,1)S(1)} %pad_maximum_fusion.3), channel_id=1, source_target_pairs={{0,8},{8,0},{16,24},{24,16},{1,9},{9,1},{17,25},{25,17},{2,10},{10... | collective-permute-start | bytes 995336 | tf_op jit(solution)/shard_map/ppermute | solution.py:23
  113.1 4.4 %collective-permute-done.20 = bf16[144,1152]{1,0:T(8,128)(2,1)} collective-permute-done((bf16[144,1152]{1,0:T(8,128)(2,1)S(1)}, bf16[144,1152]{1,0:T(8,128)(2,1)}, u32[]{:S(2)}, u32[]{:S(2)}) %collective-permute-start.20) | collective-permute-done | bytes 331808 | tf_op jit(solution)/shard_map/ppermute | solution.py:23
  117.4 3.0 %collective-permute-start.21 = (bf16[144,1152]{1,0:T(8,128)(2,1)}, bf16[144,1152]{1,0:T(8,128)(2,1)}, u32[]{:S(2)}, u32[]{:S(2)}) collective-permute-start(bf16[144,1152]{1,0:T(8,128)(2,1)} %collective-permute-done.20), channel_id=1, source_target_pairs={{0,8},{8,0},{16,24},{24,16},{1,9},{9,1},{17,25},{25,17},{2,10},{10... | collective-permute-start | bytes 995336 | tf_op jit(solution)/shard_map/ppermute | solution.py:23
  120.4 1.6 %collective-permute-done.21 = bf16[144,1152]{1,0:T(8,128)(2,1)} collective-permute-done((bf16[144,1152]{1,0:T(8,128)(2,1)}, bf16[144,1152]{1,0:T(8,128)(2,1)}, u32[]{:S(2)}, u32[]{:S(2)}) %collective-permute-start.21) | collective-permute-done | bytes 331808 | tf_op jit(solution)/shard_map/ppermute | solution.py:23
  122.0 2.3 %select_convert_fusion = (f32[144,1152]{1,0:T(8,128)}, bf16[144,1152]{1,0:T(8,128)(2,1)S(1)}, bf16[144,1152]{1,0:T(8,128)(2,1)S(1)}, bf16[144,1152]{1,0:T(8,128)(2,1)S(1)}) fusion(pred[]{:T(512)S(6)} %eq.71, bf16[144,1152]{1,0:T(8,128)(2,1)} %collective-permute-done.20, bf16[144,1152]{1,0:T(8,128)(2,1)} %collective-permute-done.21, pred[]{:T(512)S(6)} %eq.72, ...), kind=kLoop, calls=%fused_computation.105 | loop fusion | flops 2488320 | bytes 2985986 | tf_op jit(solution)/shard_map/convert_element_type | solution.py:193
  124.3 1.4 %maximum_convert_fusion = f32[144,3456]{1,0:T(8,128)} fusion(bf16[144,1152]{1,0:T(8,128)(2,1)S(1)} %get-tuple-element.35, bf16[144,1152]{1,0:T(8,128)(2,1)S(1)} %get-tuple-element.34, bf16[144,1152]{1,0:T(8,128)(2,1)S(1)} %get-tuple-element.36), kind=kLoop, calls=%fused_computation.60 | loop fusion | flops 2985984 | bytes 2985984 | tf_op jit(solution)/shard_map/convert_element_type | solution.py:192
  (104 shorter events, 5.1 us)
Async XLA Ops:
  0.6 20.9 %copy-start = (bf16[1152,1152]{1,0:T(8,128)(2,1)S(1)}, bf16[1152,1152]{1,0:T(8,128)(2,1)}, u32[]{:S(2)}) copy-start(bf16[1152,1152]{1,0:T(8,128)(2,1)} %param.13) | copy-start | bytes 7962628
  2.8 10.6 %copy-start.16 = (f32[1152]{0:T(1024)S(1)}, f32[1152]{0:T(1024)}, u32[]{:S(2)}) copy-start(f32[1152]{0:T(1024)} %param.11) | copy-start | bytes 13828
  2.8 9.8 %all-to-all-start = ((bf16[2,64,1152]{2,0,1:T(2,128)(2,1)}), bf16[2,64,1152]{2,0,1:T(2,128)(2,1)S(1)}, u32[]{:S(2)}, u32[]{:S(2)}) async-start(bf16[2,64,1152]{2,0,1:T(2,128)(2,1)} %bitcast.209), calls=%async_computation | async-start | bytes 589824 | tf_op jit(solution)/shard_map/all_to_all | solution.py:202
  21.5 1.0 copy-start.14
  21.5 1.0 copy-start.15
  23.5 2.1 %collective-permute-start = (f32[4,8]{1,0:T(4,128)S(1)}, f32[4,8]{1,0:T(4,128)S(1)}, u32[]{:S(2)}, u32[]{:S(2)}) collective-permute-start(f32[4,8]{1,0:T(4,128)S(1)} %fusion.68), channel_id=1, source_target_pairs={{0,8},{8,0},{16,24},{24,16},{1,9},{9,1},{17,25},{25,17},{2,10},{10... | collective-permute-start | bytes 392 | tf_op jit(solution)/shard_map/ppermute | solution.py:23
  25.6 2.6 %copy-start.18 = (f32[1,4,8]{2,1,0:T(4,128)S(1)}, f32[1,4,8]{2,1,0:T(4,128)}, u32[]{:S(2)}) copy-start(f32[1,4,8]{2,1,0:T(4,128)} %param.10) | copy-start | bytes 388
  25.6 2.5 %collective-permute-start.1 = (f32[4,8]{1,0:T(4,128)S(1)}, f32[4,8]{1,0:T(4,128)S(1)}, u32[]{:S(2)}, u32[]{:S(2)}) collective-permute-start(f32[4,8]{1,0:T(4,128)S(1)} %add.214), channel_id=1, source_target_pairs={{0,16},{8,24},{16,0},{24,8},{1,17},{9,25},{17,1},{25,9},{2,18},{10... | collective-permute-start | bytes 392 | tf_op jit(solution)/shard_map/ppermute | solution.py:23
  26.8 10.6 %copy-start.9 = (bf16[1152,128]{1,0:T(8,128)(2,1)}, bf16[1152,128]{1,0:T(8,128)(2,1)S(1)}, u32[]{:S(2)}) copy-start(bf16[1152,128]{1,0:T(8,128)(2,1)S(1)} %get-tuple-element.45) | copy-start | bytes 884740
  26.8 12.2 %copy-start.7 = (bf16[1152,128]{1,0:T(8,128)(2,1)}, bf16[1152,128]{1,0:T(8,128)(2,1)S(1)}, u32[]{:S(2)}) copy-start(bf16[1152,128]{1,0:T(8,128)(2,1)S(1)} %get-tuple-element.48) | copy-start | bytes 884740
  28.2 2.0 %copy-start.17 = (f32[4,8]{1,0:T(4,128)}, f32[4,8]{1,0:T(4,128)S(1)}, u32[]{:S(2)}) copy-start(f32[4,8]{1,0:T(4,128)S(1)} %add_divide_fusion) | copy-start | bytes 388
  29.3 12.4 %copy-start.1 = (bf16[128,1152]{1,0:T(8,128)(2,1)}, bf16[128,1152]{1,0:T(8,128)(2,1)S(1)}, u32[]{:S(2)}) copy-start(bf16[128,1152]{1,0:T(8,128)(2,1)S(1)} %multiply_convert_fusion) | copy-start | bytes 884740
  35.7 6.4 %collective-permute-start.6 = (bf16[8,144,384]{2,1,0:T(8,128)(2,1)S(1)}, bf16[8,144,384]{2,1,0:T(8,128)(2,1)S(1)}, u32[]{:S(2)}, u32[]{:S(2)}) collective-permute-start(bf16[8,144,384]{2,1,0:T(8,128)(2,1)S(1)} %bitcast.240), channel_id=1, source_target_pairs={{0,8},{8,0},{16,24},{24,16},{1,9},{9,1},{17,25},{25,17},{2,10},{10... | collective-permute-start | bytes 2654216 | tf_op jit(solution)/shard_map/ppermute | solution.py:23
  37.4 5.9 %collective-permute-start.7 = (bf16[8,144,384]{2,1,0:T(8,128)(2,1)S(1)}, bf16[8,144,384]{2,1,0:T(8,128)(2,1)S(1)}, u32[]{:S(2)}, u32[]{:S(2)}) collective-permute-start(bf16[8,144,384]{2,1,0:T(8,128)(2,1)S(1)} %bitcast.239), channel_id=1, source_target_pairs={{0,8},{8,0},{16,24},{24,16},{1,9},{9,1},{17,25},{25,17},{2,10},{10... | collective-permute-start | bytes 2654216 | tf_op jit(solution)/shard_map/ppermute | solution.py:23
  38.0 7.3 %collective-permute-start.4 = (bf16[8,144,384]{2,1,0:T(8,128)(2,1)S(1)}, bf16[8,144,384]{2,1,0:T(8,128)(2,1)S(1)}, u32[]{:S(2)}, u32[]{:S(2)}) collective-permute-start(bf16[8,144,384]{2,1,0:T(8,128)(2,1)S(1)} %bitcast.236), channel_id=1, source_target_pairs={{0,8},{8,0},{16,24},{24,16},{1,9},{9,1},{17,25},{25,17},{2,10},{10... | collective-permute-start | bytes 2654216 | tf_op jit(solution)/shard_map/ppermute | solution.py:23
  39.8 5.8 %collective-permute-start.5 = (bf16[8,144,384]{2,1,0:T(8,128)(2,1)S(1)}, bf16[8,144,384]{2,1,0:T(8,128)(2,1)S(1)}, u32[]{:S(2)}, u32[]{:S(2)}) collective-permute-start(bf16[8,144,384]{2,1,0:T(8,128)(2,1)S(1)} %bitcast.237), channel_id=1, source_target_pairs={{0,8},{8,0},{16,24},{24,16},{1,9},{9,1},{17,25},{25,17},{2,10},{10... | collective-permute-start | bytes 2654216 | tf_op jit(solution)/shard_map/ppermute | solution.py:23
  41.1 6.5 %collective-permute-start.3 = (bf16[8,144,384]{2,1,0:T(8,128)(2,1)S(1)}, bf16[8,144,384]{2,1,0:T(8,128)(2,1)S(1)}, u32[]{:S(2)}, u32[]{:S(2)}) collective-permute-start(bf16[8,144,384]{2,1,0:T(8,128)(2,1)S(1)} %bitcast.238), channel_id=1, source_target_pairs={{0,8},{8,0},{16,24},{24,16},{1,9},{9,1},{17,25},{25,17},{2,10},{10... | collective-permute-start | bytes 2654216 | tf_op jit(solution)/shard_map/ppermute | solution.py:23
  45.6 0.9 copy-start.3
  46.5 2.4 %copy-start.5 = (bf16[8,144,384]{2,1,0:T(8,128)(2,1)}, bf16[8,144,384]{2,1,0:T(8,128)(2,1)S(1)}, u32[]{:S(2)}) copy-start(bf16[8,144,384]{2,1,0:T(8,128)(2,1)S(1)} %fusion.8) | copy-start | bytes 2654212
  48.9 22.2 %collective-permute-start.9 = (bf16[8,144,384]{2,1,0:T(8,128)(2,1)}, bf16[8,144,384]{2,1,0:T(8,128)(2,1)}, u32[]{:S(2)}, u32[]{:S(2)}) collective-permute-start(bf16[8,144,384]{2,1,0:T(8,128)(2,1)} %pad_maximum_fusion), channel_id=1, source_target_pairs={{0,1},{1,0},{2,3},{3,2},{4,5},{5,4},{6,7},{7,6},{8,9},{9,8},{10,11... | collective-permute-start | bytes 2654216 | tf_op jit(solution)/shard_map/ppermute | solution.py:23
  50.7 1.9 %copy-start.13 = (bf16[8,144,384]{2,1,0:T(8,128)(2,1)S(1)}, bf16[8,144,384]{2,1,0:T(8,128)(2,1)}, u32[]{:S(2)}) copy-start(bf16[8,144,384]{2,1,0:T(8,128)(2,1)} %fusion.10) | copy-start | bytes 2654212
  50.7 2.0 %copy-start.2 = (bf16[128,1152]{1,0:T(8,128)(2,1)S(1)}, bf16[128,1152]{1,0:T(8,128)(2,1)}, u32[]{:S(2)}) copy-start(bf16[128,1152]{1,0:T(8,128)(2,1)} %copy-done.1) | copy-start | bytes 884740
  50.7 2.0 %copy-start.8 = (bf16[1152,128]{1,0:T(8,128)(2,1)S(1)}, bf16[1152,128]{1,0:T(8,128)(2,1)}, u32[]{:S(2)}) copy-start(bf16[1152,128]{1,0:T(8,128)(2,1)} %copy-done.7) | copy-start | bytes 884740
  50.7 2.4 %copy-start.12 = (bf16[8,144,384]{2,1,0:T(8,128)(2,1)S(1)}, bf16[8,144,384]{2,1,0:T(8,128)(2,1)}, u32[]{:S(2)}) copy-start(bf16[8,144,384]{2,1,0:T(8,128)(2,1)} %pad_maximum_fusion.1) | copy-start | bytes 2654212
  52.2 18.8 %copy-start.4 = (bf16[8,144,384]{2,1,0:T(8,128)(2,1)S(1)}, bf16[8,144,384]{2,1,0:T(8,128)(2,1)}, u32[]{:S(2)}) copy-start(bf16[8,144,384]{2,1,0:T(8,128)(2,1)} %copy-done.3) | copy-start | bytes 2654212
  52.2 18.8 %copy-start.6 = (bf16[8,144,384]{2,1,0:T(8,128)(2,1)S(1)}, bf16[8,144,384]{2,1,0:T(8,128)(2,1)}, u32[]{:S(2)}) copy-start(bf16[8,144,384]{2,1,0:T(8,128)(2,1)} %copy-done.5) | copy-start | bytes 2654212
  52.2 20.3 %collective-permute-start.2 = (bf16[8,144,384]{2,1,0:T(8,128)(2,1)S(1)}, bf16[8,144,384]{2,1,0:T(8,128)(2,1)S(1)}, u32[]{:S(2)}, u32[]{:S(2)}) collective-permute-start(bf16[8,144,384]{2,1,0:T(8,128)(2,1)S(1)} %bitcast.241), channel_id=1, source_target_pairs={{0,8},{8,0},{16,24},{24,16},{1,9},{9,1},{17,25},{25,17},{2,10},{10... | collective-permute-start | bytes 2654216 | tf_op jit(solution)/shard_map/ppermute | solution.py:23
  52.6 21.0 %collective-permute-start.8 = (bf16[8,144,384]{2,1,0:T(8,128)(2,1)S(1)}, bf16[8,144,384]{2,1,0:T(8,128)(2,1)S(1)}, u32[]{:S(2)}, u32[]{:S(2)}) collective-permute-start(bf16[8,144,384]{2,1,0:T(8,128)(2,1)S(1)} %copy-done.13), channel_id=1, source_target_pairs={{0,16},{8,24},{16,0},{24,8},{1,17},{9,25},{17,1},{25,9},{2,18},{10... | collective-permute-start | bytes 2654216 | tf_op jit(solution)/shard_map/ppermute | solution.py:23
  53.1 21.0 %collective-permute-start.10 = (bf16[8,144,384]{2,1,0:T(8,128)(2,1)S(1)}, bf16[8,144,384]{2,1,0:T(8,128)(2,1)S(1)}, u32[]{:S(2)}, u32[]{:S(2)}) collective-permute-start(bf16[8,144,384]{2,1,0:T(8,128)(2,1)S(1)} %copy-done.12), channel_id=1, source_target_pairs={{0,2},{1,3},{2,0},{3,1},{4,6},{5,7},{6,4},{7,5},{8,10},{9,11},{10,... | collective-permute-start | bytes 2654216 | tf_op jit(solution)/shard_map/ppermute | solution.py:23
  73.7 1.0 copy-start.11
  74.0 11.7 %copy-start.10 = (bf16[2,1,2,144,384]{4,3,2,1,0:T(8,128)(2,1)S(1)}, bf16[2,1,2,144,384]{4,3,2,1,0:T(8,128)(2,1)}, u32[]{:S(2)}) copy-start(bf16[2,1,2,144,384]{4,3,2,1,0:T(8,128)(2,1)} %get-tuple-element.39) | copy-start | bytes 1327108
  74.8 10.7 %collective-permute-start.11 = (bf16[4,144,384]{2,1,0:T(8,128)(2,1)S(1)}, bf16[4,144,384]{2,1,0:T(8,128)(2,1)S(1)}, u32[]{:S(2)}, u32[]{:S(2)}) collective-permute-start(bf16[4,144,384]{2,1,0:T(8,128)(2,1)S(1)} %slice_bitcast_fusion.2), channel_id=1, source_target_pairs={{0,1},{1,0},{2,3},{3,2},{4,5},{5,4},{6,7},{7,6},{8,9},{9,8},{10,11... | collective-permute-start | bytes 1327112 | tf_op jit(solution)/shard_map/ppermute | solution.py:23
  75.0 10.7 %collective-permute-start.13 = (bf16[4,144,384]{2,1,0:T(8,128)(2,1)S(1)}, bf16[4,144,384]{2,1,0:T(8,128)(2,1)S(1)}, u32[]{:S(2)}, u32[]{:S(2)}) collective-permute-start(bf16[4,144,384]{2,1,0:T(8,128)(2,1)S(1)} %fusion.13), channel_id=1, source_target_pairs={{0,16},{8,24},{16,0},{24,8},{1,17},{9,25},{17,1},{25,9},{2,18},{10... | collective-permute-start | bytes 1327112 | tf_op jit(solution)/shard_map/ppermute | solution.py:23
  75.7 10.3 %collective-permute-start.12 = (bf16[4,144,384]{2,1,0:T(8,128)(2,1)S(1)}, bf16[4,144,384]{2,1,0:T(8,128)(2,1)S(1)}, u32[]{:S(2)}, u32[]{:S(2)}) collective-permute-start(bf16[4,144,384]{2,1,0:T(8,128)(2,1)S(1)} %pad_maximum_fusion.2), channel_id=1, source_target_pairs={{0,2},{1,3},{2,0},{3,1},{4,6},{5,7},{6,4},{7,5},{8,10},{9,11},{10,... | collective-permute-start | bytes 1327112 | tf_op jit(solution)/shard_map/ppermute | solution.py:23
  86.1 4.8 %collective-permute-start.16 = (bf16[2,144,384]{2,1,0:T(8,128)(2,1)S(1)}, bf16[2,144,384]{2,1,0:T(8,128)(2,1)S(1)}, u32[]{:S(2)}, u32[]{:S(2)}) collective-permute-start(bf16[2,144,384]{2,1,0:T(8,128)(2,1)S(1)} %slice_bitcast_fusion.8), channel_id=1, source_target_pairs={{0,1},{1,0},{2,3},{3,2},{4,5},{5,4},{6,7},{7,6},{8,9},{9,8},{10,11... | collective-permute-start | bytes 663560 | tf_op jit(solution)/shard_map/ppermute | solution.py:23
  87.2 5.1 %collective-permute-start.15 = (bf16[2,144,384]{2,1,0:T(8,128)(2,1)S(1)}, bf16[2,144,384]{2,1,0:T(8,128)(2,1)S(1)}, u32[]{:S(2)}, u32[]{:S(2)}) collective-permute-start(bf16[2,144,384]{2,1,0:T(8,128)(2,1)S(1)} %fusion.26), channel_id=1, source_target_pairs={{0,16},{8,24},{16,0},{24,8},{1,17},{9,25},{17,1},{25,9},{2,18},{10... | collective-permute-start | bytes 663560 | tf_op jit(solution)/shard_map/ppermute | solution.py:23
  88.1 5.1 %collective-permute-start.14 = (bf16[2,144,384]{2,1,0:T(8,128)(2,1)S(1)}, bf16[2,144,384]{2,1,0:T(8,128)(2,1)S(1)}, u32[]{:S(2)}, u32[]{:S(2)}) collective-permute-start(bf16[2,144,384]{2,1,0:T(8,128)(2,1)S(1)} %slice_bitcast_fusion.10), channel_id=1, source_target_pairs={{0,2},{1,3},{2,0},{3,1},{4,6},{5,7},{6,4},{7,5},{8,10},{9,11},{10,... | collective-permute-start | bytes 663560 | tf_op jit(solution)/shard_map/ppermute | solution.py:23
  93.2 4.7 %collective-permute-start.17 = (bf16[1,144,384]{2,1,0:T(8,128)(2,1)S(1)}, bf16[1,144,384]{2,1,0:T(8,128)(2,1)S(1)}, u32[]{:S(2)}, u32[]{:S(2)}) collective-permute-start(bf16[1,144,384]{2,1,0:T(8,128)(2,1)S(1)} %slice_bitcast_fusion.18), channel_id=1, source_target_pairs={{0,4},{1,5},{2,6},{3,7},{4,0},{5,1},{6,2},{7,3},{8,12},{9,13},{10,... | collective-permute-start | bytes 331784 | tf_op jit(solution)/shard_map/ppermute | solution.py:23
  95.6 14.4 %collective-permute-start.18 = (bf16[1,144,384]{2,1,0:T(8,128)(2,1)S(1)}, bf16[1,144,384]{2,1,0:T(8,128)(2,1)S(1)}, u32[]{:S(2)}, u32[]{:S(2)}) collective-permute-start(bf16[1,144,384]{2,1,0:T(8,128)(2,1)S(1)} %slice_bitcast_fusion.17), channel_id=1, source_target_pairs={{0,4},{1,5},{2,6},{3,7},{4,0},{5,1},{6,2},{7,3},{8,12},{9,13},{10,... | collective-permute-start | bytes 331784 | tf_op jit(solution)/shard_map/ppermute | solution.py:23
  95.7 14.3 %collective-permute-start.19 = (bf16[1,144,384]{2,1,0:T(8,128)(2,1)S(1)}, bf16[1,144,384]{2,1,0:T(8,128)(2,1)S(1)}, u32[]{:S(2)}, u32[]{:S(2)}) collective-permute-start(bf16[1,144,384]{2,1,0:T(8,128)(2,1)S(1)} %slice_bitcast_fusion.16), channel_id=1, source_target_pairs={{0,4},{1,5},{2,6},{3,7},{4,0},{5,1},{6,2},{7,3},{8,12},{9,13},{10,... | collective-permute-start | bytes 331784 | tf_op jit(solution)/shard_map/ppermute | solution.py:23
  110.0 7.4 %collective-permute-start.20 = (bf16[144,1152]{1,0:T(8,128)(2,1)S(1)}, bf16[144,1152]{1,0:T(8,128)(2,1)}, u32[]{:S(2)}, u32[]{:S(2)}) collective-permute-start(bf16[144,1152]{1,0:T(8,128)(2,1)S(1)} %pad_maximum_fusion.3), channel_id=1, source_target_pairs={{0,16},{8,24},{16,0},{24,8},{1,17},{9,25},{17,1},{25,9},{2,18},{10... | collective-permute-start | bytes 995336 | tf_op jit(solution)/shard_map/ppermute | solution.py:23
  110.7 9.7 %collective-permute-start.22 = (bf16[144,1152]{1,0:T(8,128)(2,1)S(1)}, bf16[144,1152]{1,0:T(8,128)(2,1)}, u32[]{:S(2)}, u32[]{:S(2)}) collective-permute-start(bf16[144,1152]{1,0:T(8,128)(2,1)S(1)} %pad_maximum_fusion.3), channel_id=1, source_target_pairs={{0,8},{8,0},{16,24},{24,16},{1,9},{9,1},{17,25},{25,17},{2,10},{10... | collective-permute-start | bytes 995336 | tf_op jit(solution)/shard_map/ppermute | solution.py:23
  117.4 4.6 %collective-permute-start.21 = (bf16[144,1152]{1,0:T(8,128)(2,1)}, bf16[144,1152]{1,0:T(8,128)(2,1)}, u32[]{:S(2)}, u32[]{:S(2)}) collective-permute-start(bf16[144,1152]{1,0:T(8,128)(2,1)} %collective-permute-done.20), channel_id=1, source_target_pairs={{0,8},{8,0},{16,24},{24,16},{1,9},{9,1},{17,25},{25,17},{2,10},{10... | collective-permute-start | bytes 995336 | tf_op jit(solution)/shard_map/ppermute | solution.py:23
